TPU v7x, 32 devices: a whole 2x2x4 slice. The times are simulated.
32 devices in a mesh: cells: 4 (over y, x), genes: 8 (over z, core).
Axes of the slice: x: 2, y: 2, z: 4, core: 2. Of those that a mesh axis runs over, the one named last changes fastest.
Arguments:
- counts: bfloat16 [32768, 2560], P('cells', 'genes'), may hold values from 0 to 8, as said below
- library: float32 [32768], P('cells'), may hold values from 7 to 10
- noise: float32 [32768, 10], P('cells'), may hold values from -4 to 4
- batch_ids: int32 [32768], P('cells'), may hold values from 0 to 127
- gene_mask: int32 [2560], P('genes'), may hold values 0 or 1
- kl_weight: float32 [1], replicated, may hold values from 0.5 to 1
- enc_w: float32 [2560, 128], P('genes'), may hold values from -0.125 to 0.125
- enc_m: float32 [2560, 128], P('genes'), may hold values from -6.1035156e-05 to 6.1035156e-05
- enc_v: float32 [2560, 128], P('genes'), may hold values from 1.0172526e-11 to 4.0690104e-11
- dec_w: float32 [2, 128, 2560], P(None, None, 'genes'), may hold values from -0.5 to 0.5
- dec_m: float32 [2, 128, 2560], P(None, None, 'genes'), may hold values from -6.1035156e-05 to 6.1035156e-05
- dec_v: float32 [2, 128, 2560], P(None, None, 'genes'), may hold values from 1.0172526e-11 to 4.0690104e-11
- gene_par: float32 [3, 2560], P(None, 'genes'), may hold values from -3 to 3
- gene_m: float32 [3, 2560], P(None, 'genes'), may hold values from -0.00024414062 to 0.00024414062
- gene_v: float32 [3, 2560], P(None, 'genes'), may hold values from 1.6276042e-10 to 6.5104167e-10
- small_w: float32 [266, 128], replicated, may hold values from -3 to 3
- small_m: float32 [266, 128], replicated, may hold values from -3.0517578e-05 to 3.0517578e-05
- small_v: float32 [266, 128], replicated, may hold values from 3.0517578e-12 to 1.2207031e-11
- head_w: float32 [129, 20], replicated, may hold values from -0.5 to 0.5
- head_m: float32 [129, 20], replicated, may hold values from -0.00024414062 to 0.00024414062
- head_v: float32 [129, 20], replicated, may hold values from 1.6276042e-10 to 6.5104167e-10
- norm_par: float32 [4, 128], replicated, may hold values from 0.5 to 1.5
- norm_m: float32 [4, 128], replicated, may hold values from -0.00024414062 to 0.00024414062
- norm_v: float32 [4, 128], replicated, may hold values from 1.6276042e-10 to 6.5104167e-10
Outputs:
- enc_new: float32 [2560, 128], P('genes')
- enc_m_new: float32 [2560, 128], P('genes')
- enc_v_new: float32 [2560, 128], P('genes')
- enc_low: bfloat16 [2560, 128], P('genes')
- dec_new: float32 [2, 128, 2560], P(None, None, 'genes')
- dec_m_new: float32 [2, 128, 2560], P(None, None, 'genes')
- dec_v_new: float32 [2, 128, 2560], P(None, None, 'genes')
- dec_low: bfloat16 [2, 128, 2560], P(None, None, 'genes')
- gene_new: float32 [3, 2560], P(None, 'genes')
- gene_m_new: float32 [3, 2560], P(None, 'genes')
- gene_v_new: float32 [3, 2560], P(None, 'genes')
- small_new: float32 [266, 128], replicated
- small_m_new: float32 [266, 128], replicated
- small_v_new: float32 [266, 128], replicated
- head_new: float32 [129, 20], replicated
- head_m_new: float32 [129, 20], replicated
- head_v_new: float32 [129, 20], replicated
- norm_new: float32 [4, 128], replicated
- norm_m_new: float32 [4, 128], replicated
- norm_v_new: float32 [4, 128], replicated
- grad_norm: float32 [], replicated
- loss: float32 [32768], P(('cells', 'genes'))
Inputs may be any that keep to these rules, and one draw needn't show every extreme that they name: `counts`: whole numbers.
All inputs are finite; a program needn't handle non-finite values. No bound on the sum of `gene_mask` on one device may be relied on, other than what follows from the above.
Results may differ from a plain program's by a relative error of at most 0.0047.
Values may be sent and summed in bfloat16 or wider, within the bound.
No kernel may reach another device: no remote copies, remote signals or barrier semaphores. Data moves between devices by JAX's collectives and lax.ppermute only.
A program may use at most 192 MiB of HBM per device.

v0:
```python
import jax
import jax.numpy as jnp
from jax import lax
from jax.sharding import PartitionSpec as P

norm_epsilon = 0.001
zinb_epsilon = 1e-08
beta_one = 0.9
beta_two = 0.999
step_number = 5.0
decay_rate = 0.01
rate_genes = 0.03
rate_small = 0.2
max_norm = 0.1


def exact_dot(left, right):
    return jnp.dot(left, right, precision=lax.Precision.HIGHEST, preferred_element_type=jnp.float32)


def exact_inner(left, right):
    return lax.dot_general(
        left,
        right,
        (((0,), (0,)), ((), ())),
        precision=lax.Precision.HIGHEST,
        preferred_element_type=jnp.float32,
    )


def exact_back(left, right):
    return lax.dot_general(
        left,
        right,
        (((1,), (1,)), ((), ())),
        precision=lax.Precision.HIGHEST,
        preferred_element_type=jnp.float32,
    )


def plain_inner(left, right):
    return lax.dot_general(
        left, right, (((0,), (0,)), ((), ())), preferred_element_type=jnp.float32
    )


def plain_back(left, right):
    return lax.dot_general(
        left, right, (((1,), (1,)), ((), ())), preferred_element_type=jnp.float32
    )


def zinb_loglik(observed, log_mean, drop_logit, log_disp):
    dispersion = jnp.exp(log_disp)
    mean_rate = jnp.exp(log_mean)
    soft_drop = jax.nn.softplus(-drop_logit)
    log_disp_eps = jnp.log(dispersion + zinb_epsilon)
    log_both = jnp.log(dispersion + mean_rate + zinb_epsilon)
    drop_term = -drop_logit + dispersion * (log_disp_eps - log_both)
    case_zero = jax.nn.softplus(drop_term) - soft_drop
    case_other = (
        -soft_drop
        + drop_term
        + observed * (jnp.log(mean_rate + zinb_epsilon) - log_both)
        + lax.lgamma(observed + dispersion)
        - lax.lgamma(dispersion)
        - lax.lgamma(observed + 1.0)
    )
    return jnp.where(observed < zinb_epsilon, case_zero, case_other)


def wide_sum(values):
    return lax.psum((values[0], values[1]), ("cells", "genes"))


def norm_forward(pre_act, gain_row, shift_row, cell_total):
    stat_sums = wide_sum((jnp.sum(pre_act, 0), jnp.sum(pre_act * pre_act, 0)))
    stat_mean = stat_sums[0] / cell_total
    stat_var = stat_sums[1] / cell_total - stat_mean * stat_mean
    inv_std = lax.rsqrt(stat_var + norm_epsilon)
    centred = (pre_act - stat_mean) * inv_std
    affine = gain_row * centred + shift_row
    return (jax.nn.relu(affine), (centred, inv_std, affine > 0))


def norm_backward(gradient, saved, gain_row, cell_total):
    centred, inv_std, active = saved
    grad_affine = jnp.where(active, gradient, 0.0)
    stat_sums = wide_sum((jnp.sum(grad_affine, 0), jnp.sum(grad_affine * centred, 0)))
    grad_pre = (
        gain_row
        * inv_std
        * (grad_affine - stat_sums[0] / cell_total - centred * stat_sums[1] / cell_total)
    )
    return (grad_pre, stat_sums[1], stat_sums[0])


def adamw(weight, gradient, moment_one, moment_two, step_rate):
    moment_one = beta_one * moment_one + (1.0 - beta_one) * gradient
    moment_two = beta_two * moment_two + (1.0 - beta_two) * gradient * gradient
    fixed_one = moment_one / (1.0 - beta_one**step_number)
    fixed_two = moment_two / (1.0 - beta_two**step_number)
    update = fixed_one / (jnp.sqrt(fixed_two) + 1e-08) + decay_rate * weight
    return (weight - step_rate * update, moment_one, moment_two)


def per_device(
    counts,
    library,
    noise,
    batch_ids,
    gene_mask,
    kl_weight,
    enc_w,
    enc_m,
    enc_v,
    dec_w,
    dec_m,
    dec_v,
    gene_par,
    gene_m,
    gene_v,
    small_w,
    small_m,
    small_v,
    head_w,
    head_m,
    head_v,
    norm_par,
    norm_m,
    norm_v,
):
    rows_all = counts.shape[0]
    local_genes = counts.shape[1]
    cell_total = rows_all * lax.axis_size("cells")
    groups = lax.axis_size("genes")
    hidden = enc_w.shape[1]
    latent = head_w.shape[1] // 2
    batch_kinds = (small_w.shape[0] - latent) // 2
    log_counts = jnp.log1p(counts.astype(jnp.float32)).astype(jnp.bfloat16)
    enc_low = enc_w.astype(jnp.bfloat16)
    dec_cat = jnp.concatenate([dec_w[0], dec_w[1]], axis=1).astype(jnp.bfloat16)
    gene_keep = gene_mask > 0
    share_rows = rows_all // groups
    first_row = lax.axis_index("genes") * share_rows
    cell_rows = log_counts
    enc_part = lax.psum_scatter(
        jnp.dot(cell_rows, enc_low, preferred_element_type=jnp.float32),
        "genes",
        scatter_dimension=0,
        tiled=True,
    )
    own_batch = lax.dynamic_slice_in_dim(batch_ids, first_row, share_rows, 0)
    own_noise = lax.dynamic_slice_in_dim(noise, first_row, share_rows, 0)
    batch_table = (own_batch[:, None] == jnp.arange(batch_kinds, dtype=jnp.int32)[None, :]).astype(
        jnp.float32
    )
    pre_enc = enc_part + exact_dot(batch_table, small_w[:batch_kinds])
    hidden_enc, saved_enc = norm_forward(pre_enc, norm_par[0], norm_par[1], cell_total)
    head_out = exact_dot(hidden_enc, head_w[:hidden]) + head_w[hidden]
    latent_mean = head_out[:, :latent]
    latent_logvar = head_out[:, latent:]
    spread = jnp.exp(latent_logvar)
    latent_var = spread + 0.0001
    latent_std = jnp.sqrt(latent_var)
    latent_draw = latent_mean + latent_std * own_noise
    pre_dec = exact_dot(latent_draw, small_w[2 * batch_kinds :]) + exact_dot(
        batch_table, small_w[batch_kinds : 2 * batch_kinds]
    )
    hidden_dec, saved_dec = norm_forward(pre_dec, norm_par[2], norm_par[3], cell_total)
    hidden_low = hidden_dec.astype(jnp.bfloat16)
    hidden_all = lax.all_gather(hidden_low, "genes", axis=0, tiled=True)
    logits = jnp.dot(hidden_all, dec_cat, preferred_element_type=jnp.float32)
    score = logits[:, :local_genes] + gene_par[0]
    drop_logit = logits[:, local_genes:] + gene_par[1]
    masked = jnp.where(gene_keep, score, -1e30)
    local_top = jnp.max(masked, axis=1)
    top_logit = lax.pmax(local_top.astype(jnp.bfloat16), "genes").astype(local_top.dtype)
    local_mass = jnp.sum(jnp.where(gene_keep, jnp.exp(masked - top_logit[:, None]), 0.0), 1)
    exp_mass = lax.psum(local_mass, "genes")
    log_total = top_logit + jnp.log(exp_mass)
    log_mean = library[:, None] + score - log_total[:, None]
    block_rows = min(2048, rows_all)
    count_blocks = rows_all // block_rows
    disp_row = gene_par[2]

    def block_grad(block_args):
        block_counts, block_mean, block_drop = block_args

        def local_loss(mean_part, drop_part, disp_part):
            terms = zinb_loglik(block_counts.astype(jnp.float32), mean_part, drop_part, disp_part)
            return jnp.sum(jnp.where(gene_keep, terms, 0.0), axis=1)

        block_value, pullback = jax.vjp(local_loss, block_mean, block_drop, disp_row)
        grad_mean, grad_drop, grad_disp = pullback(
            jnp.full((block_counts.shape[0],), -1.0 / cell_total, jnp.float32)
        )
        return (block_value, grad_mean, grad_drop, grad_disp)

    block_values, grad_mean, grad_drop, grad_disp = lax.map(
        block_grad,
        (
            counts.reshape(count_blocks, block_rows, local_genes),
            log_mean.reshape(count_blocks, block_rows, local_genes),
            drop_logit.reshape(count_blocks, block_rows, local_genes),
        ),
    )
    recon_rows = block_values.reshape(rows_all)
    grad_mean = grad_mean.reshape(rows_all, local_genes)
    grad_drop = grad_drop.reshape(rows_all, local_genes)
    softmax_ratio = jnp.where(gene_keep, jnp.exp(score - log_total[:, None]), 0.0)
    back_mass, recon_cells = lax.psum((jnp.sum(grad_mean, 1), recon_rows), "genes")
    grad_score = grad_mean - softmax_ratio * back_mass[:, None]
    grad_cat = jnp.concatenate([grad_score, grad_drop], axis=1).astype(jnp.bfloat16)
    grad_dec = plain_inner(hidden_all, grad_cat)
    grad_gene = jnp.stack([jnp.sum(grad_score, 0), jnp.sum(grad_drop, 0), jnp.sum(grad_disp, 0)])
    cell_rows = grad_cat
    grad_hidden = lax.psum_scatter(
        plain_back(cell_rows, dec_cat), "genes", scatter_dimension=0, tiled=True
    )
    grad_pre_dec, gain_dec, shift_dec = norm_backward(
        grad_hidden, saved_dec, norm_par[2], cell_total
    )
    grad_latent_w = exact_inner(latent_draw, grad_pre_dec)
    grad_cov_dec = exact_inner(batch_table, grad_pre_dec)
    grad_draw = exact_back(grad_pre_dec, small_w[2 * batch_kinds :])
    kl_scale = kl_weight[0] / cell_total
    grad_lmean = grad_draw + kl_scale * latent_mean
    grad_lvar = grad_draw * own_noise * 0.5 * spread / latent_std + kl_scale * 0.5 * (
        spread - spread / latent_var
    )
    grad_head_out = jnp.concatenate([grad_lmean, grad_lvar], axis=1)
    grad_head = jnp.concatenate(
        [exact_inner(hidden_enc, grad_head_out), jnp.sum(grad_head_out, 0)[None, :]], axis=0
    )
    grad_hidden_enc = exact_back(grad_head_out, head_w[:hidden])
    grad_pre_enc, gain_enc, shift_enc = norm_backward(
        grad_hidden_enc, saved_enc, norm_par[0], cell_total
    )
    grad_cov_enc = exact_inner(batch_table, grad_pre_enc)
    grad_small = jnp.concatenate([grad_cov_enc, grad_cov_dec, grad_latent_w], axis=0)
    grad_norm_par = jnp.stack([gain_enc, shift_enc, gain_dec, shift_dec])
    grad_pre_low = grad_pre_enc.astype(jnp.bfloat16)
    diverge_rows = 0.5 * jnp.sum(
        latent_var + latent_mean * latent_mean - 1.0 - jnp.log(latent_var), axis=1
    )
    cell_rows = log_counts
    grad_enc = plain_inner(cell_rows, lax.all_gather(grad_pre_low, "genes", axis=0, tiled=True))
    grad_enc, grad_dec, grad_gene = lax.psum((grad_enc, grad_dec, grad_gene), "cells")
    grad_small, grad_head = lax.psum((grad_small, grad_head), ("cells", "genes"))
    own_recon = lax.dynamic_slice_in_dim(recon_cells, first_row, share_rows, 0)
    cell_loss = kl_weight[0] * diverge_rows - own_recon
    gene_square = (
        jnp.sum(grad_enc * grad_enc) + jnp.sum(grad_dec * grad_dec) + jnp.sum(grad_gene * grad_gene)
    )
    gene_square = lax.psum(gene_square, "genes")
    small_square = (
        jnp.sum(grad_small * grad_small)
        + jnp.sum(grad_head * grad_head)
        + jnp.sum(grad_norm_par * grad_norm_par)
    )
    norm_value = jnp.sqrt(gene_square + small_square)
    factor = jnp.minimum(1.0, max_norm / norm_value)
    grad_dec_split = jnp.stack([grad_dec[:, :local_genes], grad_dec[:, local_genes:]])
    enc_res = adamw(enc_w, grad_enc * factor, enc_m, enc_v, rate_genes)
    dec_res = adamw(dec_w, grad_dec_split * factor, dec_m, dec_v, rate_genes)
    gene_res = adamw(gene_par, grad_gene * factor, gene_m, gene_v, rate_small)
    small_res = adamw(small_w, grad_small * factor, small_m, small_v, rate_small)
    head_res = adamw(head_w, grad_head * factor, head_m, head_v, rate_small)
    norm_res = adamw(norm_par, grad_norm_par * factor, norm_m, norm_v, rate_small)
    return (
        enc_res[0],
        enc_res[1],
        enc_res[2],
        enc_res[0].astype(jnp.bfloat16),
        dec_res[0],
        dec_res[1],
        dec_res[2],
        dec_res[0].astype(jnp.bfloat16),
        gene_res[0],
        gene_res[1],
        gene_res[2],
        small_res[0],
        small_res[1],
        small_res[2],
        head_res[0],
        head_res[1],
        head_res[2],
        norm_res[0],
        norm_res[1],
        norm_res[2],
        norm_value,
        cell_loss,
    )


def solution(mesh):
    placed = (
        P("cells", "genes"),
        P("cells"),
        P("cells", None),
        P("cells"),
        P("genes"),
        P(),
        P("genes", None),
        P("genes", None),
        P("genes", None),
        P(None, None, "genes"),
        P(None, None, "genes"),
        P(None, None, "genes"),
        P(None, "genes"),
        P(None, "genes"),
        P(None, "genes"),
        P(),
        P(),
        P(),
        P(),
        P(),
        P(),
        P(),
        P(),
        P(),
    )
    return jax.shard_map(
        per_device,
        mesh=mesh,
        in_specs=placed,
        out_specs=(
            P("genes", None),
            P("genes", None),
            P("genes", None),
            P("genes", None),
            P(None, None, "genes"),
            P(None, None, "genes"),
            P(None, None, "genes"),
            P(None, None, "genes"),
            P(None, "genes"),
            P(None, "genes"),
            P(None, "genes"),
            P(),
            P(),
            P(),
            P(),
            P(),
            P(),
            P(),
            P(),
            P(),
            P(),
            P(("cells", "genes")),
        ),
        check_vma=False,
    )
```

profile of v0, /device:TPU:0, one launch (start us, length us, event | category | flops | bytes accessed | tf_op | source)
XLA Modules:
  0.0 1099.5 jit_solution(12833105348551881705)
XLA Ops:
  16.9 51.9 %reduce-scatter.3.cloned.1.call-done = f32[1024,128]{1,0:T(8,128)} async-done(((f32[8192,128]{1,0:T(8,128)}), f32[1024,128]{1,0:T(8,128)}) %reduce-scatter.3.cloned.1.call-update) | async-done | bytes 524304 | tf_op jit(solution)/shard_map/reduce_scatter | solution.py:147
  70.3 37.8 %all-reduce.3 = (f32[128]{0:T(128)S(1)}, f32[128]{0:T(128)S(1)}) all-reduce(f32[128]{0:T(128)S(1)} %get-tuple-element.381, f32[128]{0:T(128)S(1)} %get-tuple-element.380), channel_id=1, replica_groups=mesh['cells'=4,'genes'=8] {'cells','genes'}, use_global_device_ids=true, to_apply=%region_2.0 | all-reduce | flops 256 | bytes 2048 | tf_op jit(solution)/shard_map/psum | solution.py:73
  112.4 41.4 %all-reduce.2 = (f32[128]{0:T(128)S(1)}, f32[128]{0:T(128)S(1)}) all-reduce(f32[128]{0:T(128)S(1)} %get-tuple-element.379, f32[128]{0:T(128)S(1)} %get-tuple-element.378), channel_id=1, replica_groups=mesh['cells'=4,'genes'=8] {'cells','genes'}, use_global_device_ids=true, to_apply=%region_6.7 | all-reduce | flops 256 | bytes 2048 | tf_op jit(solution)/shard_map/psum | solution.py:73
  163.9 20.5 %all-gather.3.cloned.1.call-done = bf16[8192,128]{1,0:T(8,128)(2,1)} async-done(((bf16[1024,128]{1,0:T(8,128)(2,1)}), bf16[8192,128]{1,0:T(8,128)(2,1)}) %all-gather.3.cloned.1.call-update) | async-done | bytes 2097168 | tf_op jit(solution)/shard_map/all_gather | solution.py:172
  198.1 27.6 %pmax.7 = bf16[8192]{0:T(1024)(128)(2,1)S(1)} all-reduce(bf16[8192]{0:T(1024)(128)(2,1)S(1)} %select_reduce_fusion.2), channel_id=1, replica_groups=mesh['cells'=4,'genes'=8] {'genes'}, use_global_device_ids=true, to_apply=%region_10.11 | all-reduce | flops 8192 | bytes 32768 | tf_op jit(solution)/shard_map/pmax | solution.py:178
  232.7 26.2 %psum.123 = f32[8192]{0:T(1024)S(1)} all-reduce(f32[8192]{0:T(1024)S(1)} %select_reduce_fusion.1), channel_id=1, replica_groups=mesh['cells'=4,'genes'=8] {'genes'}, use_global_device_ids=true, to_apply=%region_12.13 | all-reduce | flops 8192 | bytes 65536 | tf_op jit(solution)/shard_map/psum | solution.py:180
  258.9 15.5 %add_subtract_fusion = (f32[8192,320]{0,1:T(8,128)}, f32[8192,320]{0,1:T(8,128)}) fusion(f32[8192,640]{0,1:T(8,128)} %copy-done.1, f32[8192]{0:T(1024)S(1)} %log_add_fusion, f32[320]{0:T(512)S(1)} %get-tuple-element.466, f32[8192]{0:T(1024)S(1)} %copy-done.29, f32[320]{0:T(512)S(1)} %get-tuple-element.465), kind=kLoop, calls=%fused_computation.155 | loop fusion | flops 10485760 | bytes 42011136 | tf_op jit(solution)/shard_map/sub | solution.py:182
  274.4 11.9 %copy.74 = f32[8192,320]{1,0:T(8,128)} copy(f32[8192,320]{0,1:T(8,128)} %get-tuple-element.452) | data formatting | bytes 20971520 | tf_op jit(solution)/shard_map/while | solution.py:200
  286.3 11.8 %copy.75 = f32[8192,320]{1,0:T(8,128)} copy(f32[8192,320]{0,1:T(8,128)} %get-tuple-element.451) | data formatting | bytes 20971520 | tf_op jit(solution)/shard_map/while | solution.py:200
  298.1 323.2 %while.21 = (s32[]{:T(128)}, f32[4,2048]{1,0:T(4,128)S(1)}, f32[4,2048,320]{2,1,0:T(8,128)}, f32[4,2048,320]{2,1,0:T(8,128)}, f32[4,320]{1,0:T(4,128)S(1)}, /*in...) while((s32[]{:T(128)}, f32[4,2048]{1,0:T(4,128)S(1)}, ...), condition=%wide.region_20.22_spmd, body=%wide.region_13.21_spmd.sunk | while | flops 162566592 | bytes 51453508 | solution.py:200
  305.3 64.6 %multiply_reduce_fusion.13 = (f32[320]{0:T(512)S(1)}, f32[2048]{0:T(1024)S(1)}, f32[320]{0:T(512)S(1)}, f32[320]{0:T(512)S(1)}, f32[320]{0:T(512)S(1)}) fusion(f32[2048,320]{1,0:T(8,128)S(1)} %get-tuple-element.570, f32[4,2048,320]{2,1,0:T(8,128)} %get-tuple-element.620, s32[]{:T(128)} %get-tuple-element.596, f32[320]{0:T(512)S(1)} %get-tuple-element.569, ...), kind=kLoop, calls=%fused_computation.91.clone.1 | loop fusion | flops 124515072 | bytes 9193796 | tf_op jit(solution)/shard_map/while/body/eval_jaxpr/transpose(jvp())/reduce_sum | solution.py:59
  386.1 64.6 %multiply_reduce_fusion.13 = (f32[320]{0:T(512)S(1)}, f32[2048]{0:T(1024)S(1)}, f32[320]{0:T(512)S(1)}, f32[320]{0:T(512)S(1)}, f32[320]{0:T(512)S(1)}) fusion(f32[2048,320]{1,0:T(8,128)S(1)} %get-tuple-element.570, f32[4,2048,320]{2,1,0:T(8,128)} %get-tuple-element.620, s32[]{:T(128)} %get-tuple-element.596, f32[320]{0:T(512)S(1)} %get-tuple-element.569, ...), kind=kLoop, calls=%fused_computation.91.clone.1 | loop fusion | flops 124515072 | bytes 9193796 | tf_op jit(solution)/shard_map/while/body/eval_jaxpr/transpose(jvp())/reduce_sum | solution.py:59
  466.9 64.6 %multiply_reduce_fusion.13 = (f32[320]{0:T(512)S(1)}, f32[2048]{0:T(1024)S(1)}, f32[320]{0:T(512)S(1)}, f32[320]{0:T(512)S(1)}, f32[320]{0:T(512)S(1)}) fusion(f32[2048,320]{1,0:T(8,128)S(1)} %get-tuple-element.570, f32[4,2048,320]{2,1,0:T(8,128)} %get-tuple-element.620, s32[]{:T(128)} %get-tuple-element.596, f32[320]{0:T(512)S(1)} %get-tuple-element.569, ...), kind=kLoop, calls=%fused_computation.91.clone.1 | loop fusion | flops 124515072 | bytes 9193796 | tf_op jit(solution)/shard_map/while/body/eval_jaxpr/transpose(jvp())/reduce_sum | solution.py:59
  547.7 64.6 %multiply_reduce_fusion.13 = (f32[320]{0:T(512)S(1)}, f32[2048]{0:T(1024)S(1)}, f32[320]{0:T(512)S(1)}, f32[320]{0:T(512)S(1)}, f32[320]{0:T(512)S(1)}) fusion(f32[2048,320]{1,0:T(8,128)S(1)} %get-tuple-element.570, f32[4,2048,320]{2,1,0:T(8,128)} %get-tuple-element.620, s32[]{:T(128)} %get-tuple-element.596, f32[320]{0:T(512)S(1)} %get-tuple-element.569, ...), kind=kLoop, calls=%fused_computation.91.clone.1 | loop fusion | flops 124515072 | bytes 9193796 | tf_op jit(solution)/shard_map/while/body/eval_jaxpr/transpose(jvp())/reduce_sum | solution.py:59
  621.3 11.9 %copy.76 = f32[8192,320]{0,1:T(8,128)} copy(f32[8192,320]{1,0:T(8,128)} %bitcast.145) | data formatting | bytes 20971520 | tf_op jit(solution)/shard_map/reshape | solution.py:209
  638.9 26.4 %psum.124 = f32[8192]{0:T(1024)S(1)} all-reduce(f32[8192]{0:T(1024)S(1)} %bitcast.150), channel_id=1, replica_groups=mesh['cells'=4,'genes'=8] {'genes'}, use_global_device_ids=true, to_apply=%region_22.24 | all-reduce | flops 8192 | bytes 65536 | tf_op jit(solution)/shard_map/psum | solution.py:212
  665.3 12.6 %fusion.159 = (f32[320]{0:T(512)S(1)}, bf16[4,2048,320]{2,1,0:T(8,128)(2,1)}) fusion(f32[4,2048,320]{2,1,0:T(8,128)} %get-tuple-element.298), kind=kLoop, calls=%fused_computation.301 | loop fusion | flops 5242560 | bytes 15729920 | tf_op jit(solution)/shard_map/reduce_sum | solution.py:216
  703.0 47.4 %reduce-scatter.5.cloned.1.call-done = f32[1024,128]{1,0:T(8,128)} async-done(((f32[8192,128]{1,0:T(8,128)}), f32[1024,128]{1,0:T(8,128)}) %reduce-scatter.5.cloned.1.call-update) | async-done | bytes 524304 | tf_op jit(solution)/shard_map/reduce_scatter | solution.py:218
  751.6 37.8 %all-reduce.1 = (f32[128]{0:T(128)S(1)}, f32[128]{0:T(128)S(1)}) all-reduce(f32[128]{0:T(128)S(1)} %get-tuple-element.375, f32[128]{0:T(128)S(1)} %get-tuple-element.374), channel_id=1, replica_groups=mesh['cells'=4,'genes'=8] {'cells','genes'}, use_global_device_ids=true, to_apply=%region_27.29 | all-reduce | flops 256 | bytes 2048 | tf_op jit(solution)/shard_map/psum | solution.py:73
  794.5 41.7 %all-reduce = (f32[128]{0:T(128)S(1)}, f32[128]{0:T(128)S(1)}, f32[129,20]{0,1:T(8,128)S(1)}) all-reduce(f32[128]{0:T(128)S(1)} %get-tuple-element.377, f32[128]{0:T(128)S(1)} %get-tuple-element.376, f32[129,20]{0,1:T(8,128)S(1)} %pad_maximum_fusion.10), channel_id=1, replica_groups=mesh['cells'=4,'genes'=8] {'cells','genes'}, use_global_device_ids=true, to_apply=%region_31.33 | all-reduce | flops 2836 | bytes 22688 | tf_op jit(solution)/shard_map/psum | solution.py:73
  848.7 17.6 %all-gather.5.cloned.1.call-done = bf16[8192,128]{1,0:T(8,128)(2,1)} async-done(((bf16[1024,128]{1,0:T(8,128)(2,1)}), bf16[8192,128]{1,0:T(8,128)(2,1)}) %all-gather.5.cloned.1.call-update) | async-done | bytes 2097168 | tf_op jit(solution)/shard_map/all_gather | solution.py:248
  886.3 105.8 %all-reduce.9.cloned.1.call-done = f32[266,128]{1,0:T(8,128)} async-done(((f32[266,128]{1,0:T(8,128)}), f32[266,128]{1,0:T(8,128)}) %all-reduce.9.cloned.1.call-update) | async-done | bytes 136208 | tf_op jit(solution)/shard_map/psum | solution.py:250
  995.5 47.6 %all-reduce.11.cloned.1.call-done = (f32[320,128]{1,0:T(8,128)}, f32[128,640]{1,0:T(8,128)}) async-done(((f32[320,128]{1,0:T(8,128)}, f32[128,640]{1,0:T(8,128)}), (f32[320,128]{1,0:T(8,128)}, f32[128,640]{1,0:T(8,128)})) %all-reduce.11.cloned.1.call-update) | async-done | bytes 491536 | tf_op jit(solution)/shard_map/psum | solution.py:249
  1049.5 29.1 %all-reduce.4 = (f32[]{:T(128)}, f32[8192]{0:T(1024)}) all-reduce(f32[]{:T(128)S(6)} %add.455, f32[8192]{0:T(1024)S(1)} %bitcast.149), channel_id=1, replica_groups=mesh['cells'=4,'genes'=8] {'genes'}, use_global_device_ids=true, to_apply=%region_41.43 | all-reduce | flops 8193 | bytes 65544 | tf_op jit(solution)/shard_map/psum | solution.py:256
  (246 shorter events, 196.7 us)
Async XLA Ops:
  7.2 61.6 %reduce-scatter.3.cloned.1.call-start = ((), (), s32[]{:S(2)}) async-start(), calls=%async_computation.2 | async-start | bytes 4718592 | tf_op jit(solution)/shard_map/reduce_scatter | solution.py:147
  15.9 168.4 %all-gather.3.cloned.1.call-start = ((), (), s32[]{:S(2)}) async-start(), calls=%async_computation.3 | async-start | bytes 2359296 | tf_op jit(solution)/shard_map/all_gather | solution.py:172
  16.7 138.7 %copy-start.23 = (s32[1024]{0:T(1024)}, s32[1024]{0:T(1024)S(1)}, u32[]{:S(2)}) copy-start(s32[1024]{0:T(1024)S(1)} %dynamic_slice.41) | copy-start | bytes 12292
  16.9 138.6 %copy-start.37 = (f32[128]{0:T(128)}, f32[128]{0:T(128)S(1)}, u32[]{:S(2)}) copy-start(f32[128]{0:T(128)S(1)} %get-tuple-element.469) | copy-start | bytes 1540
  16.9 138.6 %copy-start.39 = (f32[128]{0:T(128)}, f32[128]{0:T(128)S(1)}, u32[]{:S(2)}) copy-start(f32[128]{0:T(128)S(1)} %get-tuple-element.472) | copy-start | bytes 1540
  16.9 138.6 %copy-start.52 = (f32[128]{0:T(128)}, f32[128]{0:T(128)S(1)}, u32[]{:S(2)}) copy-start(f32[128]{0:T(128)S(1)} %get-tuple-element.470) | copy-start | bytes 1540
  16.9 138.6 %copy-start.54 = (f32[128]{0:T(128)}, f32[128]{0:T(128)S(1)}, u32[]{:S(2)}) copy-start(f32[128]{0:T(128)S(1)} %get-tuple-element.471) | copy-start | bytes 1540
  155.2 595.2 %reduce-scatter.5.cloned.1.call-start = ((), (), s32[]{:S(2)}) async-start(), calls=%async_computation.4 | async-start | bytes 4718592 | tf_op jit(solution)/shard_map/reduce_scatter | solution.py:218
  702.0 87.4 %copy-start.48 = (f32[128]{0:T(128)S(1)}, f32[128]{0:T(128)}, u32[]{:S(2)}) copy-start(f32[128]{0:T(128)} %get-tuple-element.468) | copy-start | bytes 1540
  702.0 88.7 %copy-start.13 = (f32[266,128]{1,0:T(8,128)S(1)}, f32[266,128]{1,0:T(8,128)}, u32[]{:S(2)}) copy-start(f32[266,128]{1,0:T(8,128)} %param.42) | copy-start | bytes 408580
  702.0 88.7 %copy-start.18 = (f32[1024,20]{0,1:T(8,128)S(1)}, f32[1024,20]{0,1:T(8,128)}, u32[]{:S(2)}) copy-start(f32[1024,20]{0,1:T(8,128)} %copy-done.17) | copy-start | bytes 245764
  702.0 90.7 %copy-start.7 = (f32[1024,128]{1,0:T(8,128)S(1)}, f32[1024,128]{1,0:T(8,128)}, u32[]{:S(2)}) copy-start(f32[1024,128]{1,0:T(8,128)} %copy-done.6) | copy-start | bytes 1572868
  702.0 90.6 %copy-start.45 = (f32[128]{0:T(128)S(1)}, f32[128]{0:T(128)}, u32[]{:S(2)}) copy-start(f32[128]{0:T(128)} %copy-done.44) | copy-start | bytes 1540
  702.0 90.6 %copy-start.47 = (f32[128]{0:T(128)S(1)}, f32[128]{0:T(128)}, u32[]{:S(2)}) copy-start(f32[128]{0:T(128)} %copy-done.46) | copy-start | bytes 1540
  702.1 90.6 %copy-start.53 = (f32[128]{0:T(128)S(1)}, f32[128]{0:T(128)}, u32[]{:S(2)}) copy-start(f32[128]{0:T(128)} %copy-done.52) | copy-start | bytes 1540
  702.1 90.6 %copy-start.55 = (f32[128]{0:T(128)S(1)}, f32[128]{0:T(128)}, u32[]{:S(2)}) copy-start(f32[128]{0:T(128)} %copy-done.54) | copy-start | bytes 1540
  702.1 91.2 %copy-start.28 = (f32[129,20]{0,1:T(8,128)S(1)}, f32[129,20]{0,1:T(8,128)}, u32[]{:S(2)}) copy-start(f32[129,20]{0,1:T(8,128)} %param.45) | copy-start | bytes 30964
  702.1 134.1 %copy-start.43 = (f32[128]{0:T(128)S(1)}, f32[128]{0:T(128)}, u32[]{:S(2)}) copy-start(f32[128]{0:T(128)} %get-tuple-element.467) | copy-start | bytes 1540
  702.1 164.1 %all-gather.5.cloned.1.call-start = ((), (), s32[]{:S(2)}) async-start(), calls=%async_computation.5 | async-start | bytes 2359296 | tf_op jit(solution)/shard_map/all_gather | solution.py:248
  789.4 95.6 %copy-start.42 = (f32[128]{0:T(128)}, f32[128]{0:T(128)S(1)}, u32[]{:S(2)}) copy-start(f32[128]{0:T(128)S(1)} %get-tuple-element.411) | copy-start | bytes 1540
  789.4 95.6 %copy-start.50 = (f32[128]{0:T(128)}, f32[128]{0:T(128)S(1)}, u32[]{:S(2)}) copy-start(f32[128]{0:T(128)S(1)} %get-tuple-element.412) | copy-start | bytes 1540
  837.1 154.9 %all-reduce.9.cloned.1.call-start = ((), (), s32[]{:S(2)}) async-start(), calls=%async_computation.6 | async-start | bytes 278528 | tf_op jit(solution)/shard_map/psum | solution.py:250
  848.6 194.5 %all-reduce.11.cloned.1.call-start = ((), (), s32[]{:S(2)}) async-start(), calls=%async_computation.7 | async-start | bytes 983040 | tf_op jit(solution)/shard_map/psum | solution.py:249
  884.4 194.9 %copy-start.26 = (f32[3,320]{1,0:T(4,128)}, f32[3,320]{1,0:T(4,128)S(1)}, u32[]{:S(2)}) copy-start(f32[3,320]{1,0:T(4,128)S(1)} %psum.131) | copy-start | bytes 11524
  (41 other events, 1097.8 us)
Sparse Core Ops, SparseCore 0:
  16.1 52.6 reduce-scatter.2
  155.3 29.0 all-gather.2
  702.2 48.0 reduce-scatter.4
  837.2 29.0 all-gather.4
  872.2 119.7 all-reduce.8
  995.5 47.5 all-reduce.10
where the time goes:
time: 1110 us; the launch traced here: 1100 us
  other arithmetic  396 us (36%)
  waiting for transfers between devices  291 us (26%)
  blocking collectives  278 us (25%)
  local copies, waits for them, and re-layouts  69.4 us (6%)
  matrix products  42.9 us (4%)
  between operations  21.7 us (2%)
    reduce_sum x4, other arithmetic, zinb_loglik(): drop_term = -drop_logit + dispersion * (log_disp_eps - log_both)  259 us
    psum x4, blocking collectives, wide_sum(): return lax.psum((values[0], values[1]), ('cells', 'genes'))  159 us
    psum x1, waiting for transfers between devices, per_device(): lax.psum((grad_small, grad_head), ('cells', 'genes'))  106 us
    reduce_scatter x1, waiting for transfers between devices, per_device(): lax.psum_scatter(jnp.dot(cell_rows, enc_low, preferred_element_type=jnp.f...  51.9 us
    psum x1, waiting for transfers between devices, per_device(): lax.psum((grad_enc, grad_dec, grad_gene), 'cells')  47.6 us
    reduce_scatter x1, waiting for transfers between devices, per_device(): lax.psum_scatter(plain_back(cell_rows, dec_cat), 'genes', scatter_dimensi...  47.4 us
    dynamic_update_slice x4, other arithmetic, per_device(): lax.map(block_grad, (counts.reshape(count_blocks, block_rows, local_genes...  34.7 us
    psum x1, blocking collectives, per_device(): gene_square = lax.psum(gene_square, 'genes')  29.1 us
  transfers between devices with their start and end apart: 6, of which 6 were waited for; matrix products, arithmetic and copies ran while one was open for 3% of the time, Pallas kernels for 0%

commit v1 on v0

--- a/solution.py
+++ b/solution.py
@@ -70,7 +70,7 @@
 
 
 def wide_sum(values):
-    return lax.psum((values[0], values[1]), ("cells", "genes"))
+    return lax.psum(lax.psum((values[0], values[1]), "genes"), "cells")
 
 
 def norm_forward(pre_act, gain_row, shift_row, cell_total):

time: 1110 us -> 1030 us (0.928)
  blocking collectives: 278 us -> 240 us
  waiting for transfers between devices: 291 us -> 254 us
    psum x5 -> x9, blocking collectives: 169 us -> 131 us  [the longest x8 90.6 us: wide_sum(): return lax.psum(lax.psum((values[0], values[1]), 'genes'), 'cells')]
    psum x1, waiting for transfers between devices: 106 us -> 75.3 us  [per_device(): lax.psum((grad_small, grad_head), ('cells', 'genes'))]
where the time goes in v1:
time: 1030 us
  other arithmetic  396 us (38%)
  waiting for transfers between devices  254 us (25%)
  blocking collectives  240 us (23%)
  local copies, waits for them, and re-layouts  69.4 us (7%)
  matrix products  43.1 us (4%)
  between operations  22 us (2%)
    reduce_sum x4, other arithmetic, zinb_loglik(): drop_term = -drop_logit + dispersion * (log_disp_eps - log_both)  259 us
    psum x8, blocking collectives, wide_sum(): return lax.psum(lax.psum((values[0], values[1]), 'genes'), 'cells')  90.6 us
    psum x1, waiting for transfers between devices, per_device(): lax.psum((grad_small, grad_head), ('cells', 'genes'))  75.3 us
    reduce_scatter x1, waiting for transfers between devices, per_device(): lax.psum_scatter(jnp.dot(cell_rows, enc_low, preferred_element_type=jnp.f...  51.9 us
    psum x1, waiting for transfers between devices, per_device(): lax.psum((grad_enc, grad_dec, grad_gene), 'cells')  47.6 us
    reduce_scatter x1, waiting for transfers between devices, per_device(): lax.psum_scatter(plain_back(cell_rows, dec_cat), 'genes', scatter_dimensi...  47.3 us
    psum x1, blocking collectives, per_device(): lax.psum((grad_small, grad_head), ('cells', 'genes'))  40.3 us
    dynamic_update_slice x4, other arithmetic, per_device(): lax.map(block_grad, (counts.reshape(count_blocks, block_rows, local_genes...  34.7 us
  transfers between devices with their start and end apart: 6, of which 6 were waited for; matrix products, arithmetic and copies ran while one was open for 3% of the time, Pallas kernels for 0%

profile of v1, /device:TPU:0, one launch (start us, length us, event | category | flops | bytes accessed | tf_op | source)
XLA Modules:
  0.0 1025.7 jit_solution(7060303458582121681)
XLA Ops:
  16.9 51.9 %reduce-scatter.3.cloned.1.call-done = f32[1024,128]{1,0:T(8,128)} async-done(((f32[8192,128]{1,0:T(8,128)}), f32[1024,128]{1,0:T(8,128)}) %reduce-scatter.3.cloned.1.call-update) | async-done | bytes 524304 | tf_op jit(solution)/shard_map/reduce_scatter | solution.py:147
  70.3 13.8 %all-reduce.4 = (f32[128]{0:T(128)S(1)}, f32[128]{0:T(128)S(1)}) all-reduce(f32[128]{0:T(128)S(1)} %get-tuple-element.381, f32[128]{0:T(128)S(1)} %get-tuple-element.380), channel_id=1, replica_groups=mesh['cells'=4,'genes'=8] {'genes'}, use_global_device_ids=true, to_apply=%region_2.0 | all-reduce | flops 256 | bytes 2048 | tf_op jit(solution)/shard_map/psum | solution.py:73
  98.2 13.6 %all-reduce.3 = (f32[128]{0:T(128)S(1)}, f32[128]{0:T(128)S(1)}) all-reduce(f32[128]{0:T(128)S(1)} %get-tuple-element.379, f32[128]{0:T(128)S(1)} %get-tuple-element.378), channel_id=1, replica_groups=mesh['cells'=4,'genes'=8] {'genes'}, use_global_device_ids=true, to_apply=%region_8.9 | all-reduce | flops 256 | bytes 2048 | tf_op jit(solution)/shard_map/psum | solution.py:73
  130.1 17.6 %all-gather.3.cloned.1.call-done = bf16[8192,128]{1,0:T(8,128)(2,1)} async-done(((bf16[1024,128]{1,0:T(8,128)(2,1)}), bf16[8192,128]{1,0:T(8,128)(2,1)}) %all-gather.3.cloned.1.call-update) | async-done | bytes 2097168 | tf_op jit(solution)/shard_map/all_gather | solution.py:172
  161.4 27.6 %pmax.7 = bf16[8192]{0:T(1024)(128)(2,1)S(1)} all-reduce(bf16[8192]{0:T(1024)(128)(2,1)S(1)} %select_reduce_fusion.2), channel_id=1, replica_groups=mesh['cells'=4,'genes'=8] {'genes'}, use_global_device_ids=true, to_apply=%region_14.15 | all-reduce | flops 8192 | bytes 32768 | tf_op jit(solution)/shard_map/pmax | solution.py:178
  196.0 26.1 %psum.183 = f32[8192]{0:T(1024)S(1)} all-reduce(f32[8192]{0:T(1024)S(1)} %select_reduce_fusion.1), channel_id=1, replica_groups=mesh['cells'=4,'genes'=8] {'genes'}, use_global_device_ids=true, to_apply=%region_16.17 | all-reduce | flops 8192 | bytes 65536 | tf_op jit(solution)/shard_map/psum | solution.py:180
  222.2 15.5 %add_subtract_fusion = (f32[8192,320]{0,1:T(8,128)}, f32[8192,320]{0,1:T(8,128)}) fusion(f32[8192,640]{0,1:T(8,128)} %copy-done.1, f32[8192]{0:T(1024)S(1)} %log_add_fusion, f32[320]{0:T(512)S(1)} %get-tuple-element.474, f32[8192]{0:T(1024)S(1)} %copy-done.28, f32[320]{0:T(512)S(1)} %get-tuple-element.473), kind=kLoop, calls=%fused_computation.155 | loop fusion | flops 10485760 | bytes 42011136 | tf_op jit(solution)/shard_map/sub | solution.py:182
  237.7 11.9 %copy.74 = f32[8192,320]{1,0:T(8,128)} copy(f32[8192,320]{0,1:T(8,128)} %get-tuple-element.460) | data formatting | bytes 20971520 | tf_op jit(solution)/shard_map/while | solution.py:200
  261.4 323.2 %while.21 = (s32[]{:T(128)}, f32[4,2048]{1,0:T(4,128)S(1)}, f32[4,2048,320]{2,1,0:T(8,128)}, f32[4,2048,320]{2,1,0:T(8,128)}, f32[4,320]{1,0:T(4,128)S(1)}, /*in...) while((s32[]{:T(128)}, f32[4,2048]{1,0:T(4,128)S(1)}, ...), condition=%wide.region_24.26_spmd, body=%wide.region_17.25_spmd.sunk | while | flops 162566592 | bytes 51453508 | solution.py:200
  268.6 64.6 %multiply_reduce_fusion.13 = (f32[320]{0:T(512)S(1)}, f32[2048]{0:T(1024)S(1)}, f32[320]{0:T(512)S(1)}, f32[320]{0:T(512)S(1)}, f32[320]{0:T(512)S(1)}) fusion(f32[2048,320]{1,0:T(8,128)S(1)} %get-tuple-element.578, f32[4,2048,320]{2,1,0:T(8,128)} %get-tuple-element.628, s32[]{:T(128)} %get-tuple-element.604, f32[320]{0:T(512)S(1)} %get-tuple-element.577, ...), kind=kLoop, calls=%fused_computation.91.clone.1 | loop fusion | flops 124515072 | bytes 9193796 | tf_op jit(solution)/shard_map/while/body/eval_jaxpr/transpose(jvp())/reduce_sum | solution.py:59
  349.3 64.6 %multiply_reduce_fusion.13 = (f32[320]{0:T(512)S(1)}, f32[2048]{0:T(1024)S(1)}, f32[320]{0:T(512)S(1)}, f32[320]{0:T(512)S(1)}, f32[320]{0:T(512)S(1)}) fusion(f32[2048,320]{1,0:T(8,128)S(1)} %get-tuple-element.578, f32[4,2048,320]{2,1,0:T(8,128)} %get-tuple-element.628, s32[]{:T(128)} %get-tuple-element.604, f32[320]{0:T(512)S(1)} %get-tuple-element.577, ...), kind=kLoop, calls=%fused_computation.91.clone.1 | loop fusion | flops 124515072 | bytes 9193796 | tf_op jit(solution)/shard_map/while/body/eval_jaxpr/transpose(jvp())/reduce_sum | solution.py:59
  430.2 64.6 %multiply_reduce_fusion.13 = (f32[320]{0:T(512)S(1)}, f32[2048]{0:T(1024)S(1)}, f32[320]{0:T(512)S(1)}, f32[320]{0:T(512)S(1)}, f32[320]{0:T(512)S(1)}) fusion(f32[2048,320]{1,0:T(8,128)S(1)} %get-tuple-element.578, f32[4,2048,320]{2,1,0:T(8,128)} %get-tuple-element.628, s32[]{:T(128)} %get-tuple-element.604, f32[320]{0:T(512)S(1)} %get-tuple-element.577, ...), kind=kLoop, calls=%fused_computation.91.clone.1 | loop fusion | flops 124515072 | bytes 9193796 | tf_op jit(solution)/shard_map/while/body/eval_jaxpr/transpose(jvp())/reduce_sum | solution.py:59
  511.0 64.6 %multiply_reduce_fusion.13 = (f32[320]{0:T(512)S(1)}, f32[2048]{0:T(1024)S(1)}, f32[320]{0:T(512)S(1)}, f32[320]{0:T(512)S(1)}, f32[320]{0:T(512)S(1)}) fusion(f32[2048,320]{1,0:T(8,128)S(1)} %get-tuple-element.578, f32[4,2048,320]{2,1,0:T(8,128)} %get-tuple-element.628, s32[]{:T(128)} %get-tuple-element.604, f32[320]{0:T(512)S(1)} %get-tuple-element.577, ...), kind=kLoop, calls=%fused_computation.91.clone.1 | loop fusion | flops 124515072 | bytes 9193796 | tf_op jit(solution)/shard_map/while/body/eval_jaxpr/transpose(jvp())/reduce_sum | solution.py:59
  584.6 11.9 %copy.76 = f32[8192,320]{0,1:T(8,128)} copy(f32[8192,320]{1,0:T(8,128)} %bitcast.145) | data formatting | bytes 20971520 | tf_op jit(solution)/shard_map/reshape | solution.py:209
  602.2 26.2 %psum.184 = f32[8192]{0:T(1024)S(1)} all-reduce(f32[8192]{0:T(1024)S(1)} %bitcast.150), channel_id=1, replica_groups=mesh['cells'=4,'genes'=8] {'genes'}, use_global_device_ids=true, to_apply=%region_26.28 | all-reduce | flops 8192 | bytes 65536 | tf_op jit(solution)/shard_map/psum | solution.py:212
  628.4 12.6 %fusion.159 = (f32[320]{0:T(512)S(1)}, bf16[4,2048,320]{2,1,0:T(8,128)(2,1)}) fusion(f32[4,2048,320]{2,1,0:T(8,128)} %get-tuple-element.298), kind=kLoop, calls=%fused_computation.301 | loop fusion | flops 5242560 | bytes 15729920 | tf_op jit(solution)/shard_map/reduce_sum | solution.py:216
  666.2 47.3 %reduce-scatter.5.cloned.1.call-done = f32[1024,128]{1,0:T(8,128)} async-done(((f32[8192,128]{1,0:T(8,128)}), f32[1024,128]{1,0:T(8,128)}) %reduce-scatter.5.cloned.1.call-update) | async-done | bytes 524304 | tf_op jit(solution)/shard_map/reduce_scatter | solution.py:218
  714.7 13.9 %all-reduce.2 = (f32[128]{0:T(128)S(1)}, f32[128]{0:T(128)S(1)}) all-reduce(f32[128]{0:T(128)S(1)} %get-tuple-element.375, f32[128]{0:T(128)S(1)} %get-tuple-element.374), channel_id=1, replica_groups=mesh['cells'=4,'genes'=8] {'genes'}, use_global_device_ids=true, to_apply=%region_32.34 | all-reduce | flops 256 | bytes 2048 | tf_op jit(solution)/shard_map/psum | solution.py:73
  742.9 13.6 %all-reduce.1 = (f32[128]{0:T(128)S(1)}, f32[128]{0:T(128)S(1)}) all-reduce(f32[128]{0:T(128)S(1)} %get-tuple-element.377, f32[128]{0:T(128)S(1)} %get-tuple-element.376), channel_id=1, replica_groups=mesh['cells'=4,'genes'=8] {'genes'}, use_global_device_ids=true, to_apply=%region_38.40 | all-reduce | flops 256 | bytes 2048 | tf_op jit(solution)/shard_map/psum | solution.py:73
  777.9 14.2 %all-gather.5.cloned.1.call-done = bf16[8192,128]{1,0:T(8,128)(2,1)} async-done(((bf16[1024,128]{1,0:T(8,128)(2,1)}), bf16[8192,128]{1,0:T(8,128)(2,1)}) %all-gather.5.cloned.1.call-update) | async-done | bytes 2097168 | tf_op jit(solution)/shard_map/all_gather | solution.py:248
  801.0 40.3 %psum.198 = f32[129,20]{0,1:T(8,128)S(1)} all-reduce(f32[129,20]{0,1:T(8,128)S(1)} %pad_maximum_fusion.10), channel_id=1, replica_groups=mesh['cells'=4,'genes'=8] {'cells','genes'}, use_global_device_ids=true, to_apply=%region_53.55 | all-reduce | flops 2580 | bytes 20640 | tf_op jit(solution)/shard_map/psum | solution.py:250
  842.5 75.3 %all-reduce.13.cloned.1.call-done = f32[266,128]{1,0:T(8,128)} async-done(((f32[266,128]{1,0:T(8,128)}), f32[266,128]{1,0:T(8,128)}) %all-reduce.13.cloned.1.call-update) | async-done | bytes 136208 | tf_op jit(solution)/shard_map/psum | solution.py:250
  921.4 47.6 %all-reduce.15.cloned.1.call-done = (f32[320,128]{1,0:T(8,128)}, f32[128,640]{1,0:T(8,128)}) async-done(((f32[320,128]{1,0:T(8,128)}, f32[128,640]{1,0:T(8,128)}), (f32[320,128]{1,0:T(8,128)}, f32[128,640]{1,0:T(8,128)})) %all-reduce.15.cloned.1.call-update) | async-done | bytes 491536 | tf_op jit(solution)/shard_map/psum | solution.py:249
  975.4 29.1 %all-reduce = (f32[]{:T(128)}, f32[8192]{0:T(1024)}) all-reduce(f32[]{:T(128)S(6)} %add.471, f32[8192]{0:T(1024)S(1)} %bitcast.149), channel_id=1, replica_groups=mesh['cells'=4,'genes'=8] {'genes'}, use_global_device_ids=true, to_apply=%region_49.51 | all-reduce | flops 8193 | bytes 65544 | tf_op jit(solution)/shard_map/psum | solution.py:256
  (250 shorter events, 234.9 us)
Async XLA Ops:
  7.2 61.6 %reduce-scatter.3.cloned.1.call-start = ((), (), s32[]{:S(2)}) async-start(), calls=%async_computation.2 | async-start | bytes 4718592 | tf_op jit(solution)/shard_map/reduce_scatter | solution.py:147
  15.9 131.7 %all-gather.3.cloned.1.call-start = ((), (), s32[]{:S(2)}) async-start(), calls=%async_computation.3 | async-start | bytes 2359296 | tf_op jit(solution)/shard_map/all_gather | solution.py:172
  16.7 104.9 %copy-start.24 = (s32[1024]{0:T(1024)}, s32[1024]{0:T(1024)S(1)}, u32[]{:S(2)}) copy-start(s32[1024]{0:T(1024)S(1)} %dynamic_slice.41) | copy-start | bytes 12292
  16.9 104.8 %copy-start.37 = (f32[128]{0:T(128)}, f32[128]{0:T(128)S(1)}, u32[]{:S(2)}) copy-start(f32[128]{0:T(128)S(1)} %get-tuple-element.477) | copy-start | bytes 1540
  16.9 104.8 %copy-start.39 = (f32[128]{0:T(128)}, f32[128]{0:T(128)S(1)}, u32[]{:S(2)}) copy-start(f32[128]{0:T(128)S(1)} %get-tuple-element.480) | copy-start | bytes 1540
  16.9 104.8 %copy-start.52 = (f32[128]{0:T(128)}, f32[128]{0:T(128)S(1)}, u32[]{:S(2)}) copy-start(f32[128]{0:T(128)S(1)} %get-tuple-element.478) | copy-start | bytes 1540
  16.9 104.8 %copy-start.54 = (f32[128]{0:T(128)}, f32[128]{0:T(128)S(1)}, u32[]{:S(2)}) copy-start(f32[128]{0:T(128)S(1)} %get-tuple-element.479) | copy-start | bytes 1540
  121.1 592.4 %reduce-scatter.5.cloned.1.call-start = ((), (), s32[]{:S(2)}) async-start(), calls=%async_computation.4 | async-start | bytes 4718592 | tf_op jit(solution)/shard_map/reduce_scatter | solution.py:218
  665.1 73.4 %copy-start.48 = (f32[128]{0:T(128)S(1)}, f32[128]{0:T(128)}, u32[]{:S(2)}) copy-start(f32[128]{0:T(128)} %get-tuple-element.476) | copy-start | bytes 1540
  665.1 74.7 %copy-start.13 = (f32[266,128]{1,0:T(8,128)S(1)}, f32[266,128]{1,0:T(8,128)}, u32[]{:S(2)}) copy-start(f32[266,128]{1,0:T(8,128)} %param.42) | copy-start | bytes 408580
  665.1 74.7 %copy-start.18 = (f32[1024,20]{0,1:T(8,128)S(1)}, f32[1024,20]{0,1:T(8,128)}, u32[]{:S(2)}) copy-start(f32[1024,20]{0,1:T(8,128)} %copy-done.17) | copy-start | bytes 245764
  665.1 76.7 %copy-start.7 = (f32[1024,128]{1,0:T(8,128)S(1)}, f32[1024,128]{1,0:T(8,128)}, u32[]{:S(2)}) copy-start(f32[1024,128]{1,0:T(8,128)} %copy-done.6) | copy-start | bytes 1572868
  665.1 76.7 %copy-start.27 = (f32[129,20]{0,1:T(8,128)S(1)}, f32[129,20]{0,1:T(8,128)}, u32[]{:S(2)}) copy-start(f32[129,20]{0,1:T(8,128)} %param.45) | copy-start | bytes 30964
  665.1 76.7 %copy-start.45 = (f32[128]{0:T(128)S(1)}, f32[128]{0:T(128)}, u32[]{:S(2)}) copy-start(f32[128]{0:T(128)} %copy-done.44) | copy-start | bytes 1540
  665.1 76.7 %copy-start.47 = (f32[128]{0:T(128)S(1)}, f32[128]{0:T(128)}, u32[]{:S(2)}) copy-start(f32[128]{0:T(128)} %copy-done.46) | copy-start | bytes 1540
  665.2 76.7 %copy-start.53 = (f32[128]{0:T(128)S(1)}, f32[128]{0:T(128)}, u32[]{:S(2)}) copy-start(f32[128]{0:T(128)} %copy-done.52) | copy-start | bytes 1540
  665.2 76.7 %copy-start.55 = (f32[128]{0:T(128)S(1)}, f32[128]{0:T(128)}, u32[]{:S(2)}) copy-start(f32[128]{0:T(128)} %copy-done.54) | copy-start | bytes 1540
  665.2 99.4 %copy-start.43 = (f32[128]{0:T(128)S(1)}, f32[128]{0:T(128)}, u32[]{:S(2)}) copy-start(f32[128]{0:T(128)} %get-tuple-element.475) | copy-start | bytes 1540
  665.2 126.9 %all-gather.5.cloned.1.call-start = ((), (), s32[]{:S(2)}) async-start(), calls=%async_computation.5 | async-start | bytes 2359296 | tf_op jit(solution)/shard_map/all_gather | solution.py:248
  666.2 99.6 %copy-start.9 = (f32[2,128,320]{1,2,0:T(8,128)S(1)}, f32[2,128,320]{1,2,0:T(8,128)}, u32[]{:S(2)}) copy-start(f32[2,128,320]{1,2,0:T(8,128)} %param.36) | copy-start | bytes 983044
  764.6 76.7 %copy-start.29 = (f32[3,320]{1,0:T(4,128)}, f32[3,320]{1,0:T(4,128)S(1)}, u32[]{:S(2)}) copy-start(f32[3,320]{1,0:T(4,128)S(1)} %get-tuple-element.420) | copy-start | bytes 11524
  765.5 152.4 %all-reduce.13.cloned.1.call-start = ((), (), s32[]{:S(2)}) async-start(), calls=%async_computation.6 | async-start | bytes 278528 | tf_op jit(solution)/shard_map/psum | solution.py:250
  777.9 191.1 %all-reduce.15.cloned.1.call-start = ((), (), s32[]{:S(2)}) async-start(), calls=%async_computation.7 | async-start | bytes 983040 | tf_op jit(solution)/shard_map/psum | solution.py:249
  841.3 163.9 %copy-start.21 = (f32[129,20]{0,1:T(8,128)}, f32[129,20]{0,1:T(8,128)S(1)}, u32[]{:S(2)}) copy-start(f32[129,20]{0,1:T(8,128)S(1)} %psum.198) | copy-start | bytes 30964
  (41 other events, 1115.5 us)
Sparse Core Ops, SparseCore 0:
  16.1 52.6 reduce-scatter.2
  121.2 26.4 all-gather.2
  665.3 48.1 reduce-scatter.4
  765.6 26.4 all-gather.4
  798.1 119.7 all-reduce.12
  921.4 47.5 all-reduce.14
